TPU v7x, 32 devices: a whole 2x2x4 slice. The times are simulated.
32 devices in a mesh: blk: 8 (over z, x), rep: 4 (over y, core).
Axes of the slice: x: 2, y: 2, z: 4, core: 2. Of those that a mesh axis runs over, the one named last changes fastest.
Arguments:
- features: bfloat16 [8192, 256], P(('blk', 'rep')), may hold values from -6 to 6
- weight: bfloat16 [256, 256], replicated, may hold values from -0.375 to 0.375
- pre_cot: bfloat16 [8192, 256], P(('blk', 'rep')), may hold values from -6 to 6
- tile_count: int32 [8, 4, 8], P('blk', 'rep'), may hold values from 0 to 2, as said below
- tile_rowid: int32 [8, 4, 8, 2], P('blk', 'rep'), may hold values from 0 to 3, as said below
- edge_cols: int32 [8, 4, 8, 2, 1, 256], P('blk', 'rep'), may hold values from 0 to 255
- edge_vals: bfloat16 [8, 4, 8, 2, 1, 256], P('blk', 'rep'), may hold values from -1.25 to 1.25
Outputs:
- activations: bfloat16 [8192, 256], P(('blk', 'rep'))
- grad_weight: float32 [256, 256], replicated
Inputs may be any that keep to these rules, and one draw needn't show every extreme that they name: `tile_count`: the panel p = b always has all 2 slots live. `tile_rowid`: the 2 slots of one block row, tile position and panel name distinct row tiles.
All inputs are finite; a program needn't handle non-finite values.
Results may differ from a plain program's by a relative error of at most 0.011.
Values may be sent and summed in bfloat16 or wider, within the bound.
A program may use at most 64 MiB of HBM per device.

v0:
```python
import jax
import jax.numpy as jnp
from jax import lax
from jax.sharding import PartitionSpec as P


def shifted(array, axis, by):
    count = lax.axis_size(axis)
    return lax.ppermute(array, axis, [(i, (i + by) % count) for i in range(count)])


def shards(features, weight, pre_cot, tile_count, tile_rowid, edge_cols, edge_vals):
    tile_rows = features.shape[0]
    feat_width = features.shape[1]
    rep_count = lax.axis_size("rep")
    blocks = lax.axis_size("blk")
    home_index = lax.axis_index("blk")
    counts = tile_count.reshape(-1)
    row_ids = tile_rowid.reshape(tile_rowid.shape[2], tile_rowid.shape[3])
    edge_index = edge_cols.reshape(edge_cols.shape[2:])
    edge_weight = edge_vals.reshape(edge_vals.shape[2:])
    slot_count = edge_index.shape[1]
    columns = lax.broadcasted_iota(jnp.int32, (1, 1, 1, tile_rows), 3)
    slot_ids = jnp.arange(slot_count, dtype=jnp.int32)
    zero_weight = jnp.zeros((), jnp.bfloat16)
    totals_start = jnp.zeros((rep_count * tile_rows, feat_width), jnp.float32)

    def apply_panel(totals, panel_now, panel_index):
        index_now = lax.dynamic_index_in_dim(edge_index, panel_index, 0, keepdims=False)
        weight_now = lax.dynamic_index_in_dim(edge_weight, panel_index, 0, keepdims=False)
        dense_tiles = jnp.sum(
            jnp.where(index_now[..., None] == columns, weight_now[..., None], zero_weight), axis=1
        )
        products = jnp.einsum(
            "sij,jf->sif", dense_tiles, panel_now, preferred_element_type=jnp.float32
        )
        live_mask = (slot_ids < counts[panel_index]).astype(jnp.float32)
        slot_rows = lax.dynamic_index_in_dim(row_ids, panel_index, 0, keepdims=False)
        for slot in range(slot_count):
            row_start = slot_rows[slot] * tile_rows
            current = lax.dynamic_slice_in_dim(totals, row_start, tile_rows, 0)
            totals = lax.dynamic_update_slice_in_dim(
                totals, current + products[slot] * live_mask[slot], row_start, 0
            )
        return totals

    totals = apply_panel(totals_start, features, home_index)

    def cycle_turn(turn_index, carry):
        totals_now, panel_now = carry
        panel_now = shifted(panel_now, "blk", 1)
        totals_now = apply_panel(totals_now, panel_now, (home_index - turn_index) % blocks)
        return (totals_now, panel_now)

    totals, _ = lax.fori_loop(1, blocks, cycle_turn, (totals, features))
    summed = lax.psum_scatter(totals.astype(jnp.bfloat16), "rep", scatter_dimension=0, tiled=True)
    preact = jnp.dot(summed, weight, preferred_element_type=jnp.float32)
    activations = jnp.maximum(preact, 0.0).astype(jnp.bfloat16)
    local_grad = lax.dot_general(
        summed, pre_cot, (((0,), (0,)), ((), ())), preferred_element_type=jnp.float32
    )
    total_grad = lax.psum(local_grad, ("blk", "rep"))
    node_total = blocks * rep_count * tile_rows
    grad_weight = total_grad * node_total ** (-0.5)
    return (activations, grad_weight)


def solution(mesh):
    in_specs = (
        P(("blk", "rep"), None),
        P(),
        P(("blk", "rep"), None),
        P("blk", "rep", None),
        P("blk", "rep", None, None),
        P("blk", "rep", None, None, None, None),
        P("blk", "rep", None, None, None, None),
    )
    out_specs = (P(("blk", "rep"), None), P())
    return jax.shard_map(shards, mesh=mesh, in_specs=in_specs, out_specs=out_specs, check_vma=False)
```

profile of v0, /device:TPU:0, one launch (start us, length us, event | category | flops | bytes accessed | tf_op | source)
XLA Modules:
  0.0 244.4 jit_solution(1695783370558010207)
XLA Ops:
  7.2 0.9 copy.30
  15.6 67.5 %while.18 = (s32[]{:T(128)}, f32[1024,256]{1,0:T(8,128)S(1)}, bf16[256,256]{1,0:T(8,128)(2,1)S(1)}, s32[]{:T(128)}, s32[8,2]{0,1:T(2,128)S(1)}, /*index=5*/s32[8...) while((s32[]{:T(128)}, f32[1024,256]{1,0:T(8,128)S(1)}, ...), condition=%wide.region_1.2_spmd.clone, body=%wide.region_0.1_spmd.clone.sunk | while | flops 67633168 | bytes 3024392 | solution.py:55
  15.7 3.0 %collective-permute-start = (bf16[256,256]{1,0:T(8,128)(2,1)S(1)}, bf16[256,256]{1,0:T(8,128)(2,1)S(1)}, u32[]{:S(2)}, u32[]{:S(2)}) collective-permute-start(bf16[256,256]{1,0:T(8,128)(2,1)S(1)} %get-tuple-element.362), channel_id=1, source_target_pairs={{0,4},{4,8},{8,12},{12,16},{16,20},{20,24},{24,28},{28,0},{1,5},{5... | collective-permute-start | bytes 393224 | tf_op jit(solution)/shard_map/while/body/eval_jaxpr/ppermute | solution.py:9
  23.0 2.2 collective-permute-done
  26.1 0.7 fusion.58
  31.3 3.3 %collective-permute-done = bf16[256,256]{1,0:T(8,128)(2,1)S(1)} collective-permute-done((bf16[256,256]{1,0:T(8,128)(2,1)S(1)}, bf16[256,256]{1,0:T(8,128)(2,1)S(1)}, u32[]{:S(2)}, u32[]{:S(2)}) %collective-permute-start) | collective-permute-done | bytes 131104 | tf_op jit(solution)/shard_map/while/body/eval_jaxpr/ppermute | solution.py:9
  35.5 0.7 fusion.58
  40.7 3.3 %collective-permute-done = bf16[256,256]{1,0:T(8,128)(2,1)S(1)} collective-permute-done((bf16[256,256]{1,0:T(8,128)(2,1)S(1)}, bf16[256,256]{1,0:T(8,128)(2,1)S(1)}, u32[]{:S(2)}, u32[]{:S(2)}) %collective-permute-start) | collective-permute-done | bytes 131104 | tf_op jit(solution)/shard_map/while/body/eval_jaxpr/ppermute | solution.py:9
  44.9 0.7 fusion.58
  50.1 3.3 %collective-permute-done = bf16[256,256]{1,0:T(8,128)(2,1)S(1)} collective-permute-done((bf16[256,256]{1,0:T(8,128)(2,1)S(1)}, bf16[256,256]{1,0:T(8,128)(2,1)S(1)}, u32[]{:S(2)}, u32[]{:S(2)}) %collective-permute-start) | collective-permute-done | bytes 131104 | tf_op jit(solution)/shard_map/while/body/eval_jaxpr/ppermute | solution.py:9
  54.3 0.7 fusion.58
  59.5 3.3 %collective-permute-done = bf16[256,256]{1,0:T(8,128)(2,1)S(1)} collective-permute-done((bf16[256,256]{1,0:T(8,128)(2,1)S(1)}, bf16[256,256]{1,0:T(8,128)(2,1)S(1)}, u32[]{:S(2)}, u32[]{:S(2)}) %collective-permute-start) | collective-permute-done | bytes 131104 | tf_op jit(solution)/shard_map/while/body/eval_jaxpr/ppermute | solution.py:9
  63.7 0.7 fusion.58
  68.8 3.3 %collective-permute-done = bf16[256,256]{1,0:T(8,128)(2,1)S(1)} collective-permute-done((bf16[256,256]{1,0:T(8,128)(2,1)S(1)}, bf16[256,256]{1,0:T(8,128)(2,1)S(1)}, u32[]{:S(2)}, u32[]{:S(2)}) %collective-permute-start) | collective-permute-done | bytes 131104 | tf_op jit(solution)/shard_map/while/body/eval_jaxpr/ppermute | solution.py:9
  73.0 0.7 fusion.58
  78.2 3.3 %collective-permute-done = bf16[256,256]{1,0:T(8,128)(2,1)S(1)} collective-permute-done((bf16[256,256]{1,0:T(8,128)(2,1)S(1)}, bf16[256,256]{1,0:T(8,128)(2,1)S(1)}, u32[]{:S(2)}, u32[]{:S(2)}) %collective-permute-start) | collective-permute-done | bytes 131104 | tf_op jit(solution)/shard_map/while/body/eval_jaxpr/ppermute | solution.py:9
  82.4 0.7 fusion.58
  83.1 0.9 convert_element_type.34
  84.1 19.9 %reduce-scatter.2.cloned.1.call-done = bf16[256,256]{1,0:T(8,128)(2,1)} async-done(((bf16[1024,256]{1,0:T(8,128)(2,1)}), bf16[256,256]{1,0:T(8,128)(2,1)}) %reduce-scatter.2.cloned.1.call-update) | async-done | bytes 131088 | tf_op jit(solution)/shard_map/reduce_scatter | solution.py:56
  104.0 1.8 fusion.38
  105.8 0.9 copy-done.1
  106.8 0.8 fusion.19
  107.6 128.3 %all-reduce.2.cloned.1.call-done = f32[256,256]{1,0:T(8,128)} async-done(((f32[256,256]{1,0:T(8,128)}), f32[256,256]{1,0:T(8,128)}) %all-reduce.2.cloned.1.call-update) | async-done | bytes 262160 | tf_op jit(solution)/shard_map/psum | solution.py:62
  235.9 1.7 broadcast_multiply_fusion
  (104 shorter events, 35.4 us)
Async XLA Ops:
  7.2 96.8 %copy-start = (bf16[256,256]{1,0:T(8,128)(2,1)S(1)}, bf16[256,256]{1,0:T(8,128)(2,1)}, u32[]{:S(2)}) copy-start(bf16[256,256]{1,0:T(8,128)(2,1)} %param.11) | copy-start | bytes 393220
  7.2 96.8 %reduce-scatter.2.cloned.1.call-start = ((), (), s32[]{:S(2)}) async-start(), calls=%async_computation.1 | async-start | bytes 655360 | tf_op jit(solution)/shard_map/reduce_scatter | solution.py:56
  8.2 0.7 copy-start.3
  8.2 2.5 %copy-start.4 = (s32[1,1,8,2,1,256]{5,4,3,2,1,0:T(1,128)S(1)}, s32[1,1,8,2,1,256]{5,4,3,2,1,0:T(1,128)}, u32[]{:S(2)}) copy-start(s32[1,1,8,2,1,256]{5,4,3,2,1,0:T(1,128)} %param.14) | copy-start | bytes 49156
  10.7 0.7 copy-start.5
  15.7 9.5 %collective-permute-start = (bf16[256,256]{1,0:T(8,128)(2,1)S(1)}, bf16[256,256]{1,0:T(8,128)(2,1)S(1)}, u32[]{:S(2)}, u32[]{:S(2)}) collective-permute-start(bf16[256,256]{1,0:T(8,128)(2,1)S(1)} %get-tuple-element.362), channel_id=1, source_target_pairs={{0,4},{4,8},{8,12},{12,16},{16,20},{20,24},{24,28},{28,0},{1,5},{5... | collective-permute-start | bytes 393224 | tf_op jit(solution)/shard_map/while/body/eval_jaxpr/ppermute | solution.py:9
  26.8 7.7 %collective-permute-start = (bf16[256,256]{1,0:T(8,128)(2,1)S(1)}, bf16[256,256]{1,0:T(8,128)(2,1)S(1)}, u32[]{:S(2)}, u32[]{:S(2)}) collective-permute-start(bf16[256,256]{1,0:T(8,128)(2,1)S(1)} %get-tuple-element.362), channel_id=1, source_target_pairs={{0,4},{4,8},{8,12},{12,16},{16,20},{20,24},{24,28},{28,0},{1,5},{5... | collective-permute-start | bytes 393224 | tf_op jit(solution)/shard_map/while/body/eval_jaxpr/ppermute | solution.py:9
  36.2 7.7 %collective-permute-start = (bf16[256,256]{1,0:T(8,128)(2,1)S(1)}, bf16[256,256]{1,0:T(8,128)(2,1)S(1)}, u32[]{:S(2)}, u32[]{:S(2)}) collective-permute-start(bf16[256,256]{1,0:T(8,128)(2,1)S(1)} %get-tuple-element.362), channel_id=1, source_target_pairs={{0,4},{4,8},{8,12},{12,16},{16,20},{20,24},{24,28},{28,0},{1,5},{5... | collective-permute-start | bytes 393224 | tf_op jit(solution)/shard_map/while/body/eval_jaxpr/ppermute | solution.py:9
  45.6 7.7 %collective-permute-start = (bf16[256,256]{1,0:T(8,128)(2,1)S(1)}, bf16[256,256]{1,0:T(8,128)(2,1)S(1)}, u32[]{:S(2)}, u32[]{:S(2)}) collective-permute-start(bf16[256,256]{1,0:T(8,128)(2,1)S(1)} %get-tuple-element.362), channel_id=1, source_target_pairs={{0,4},{4,8},{8,12},{12,16},{16,20},{20,24},{24,28},{28,0},{1,5},{5... | collective-permute-start | bytes 393224 | tf_op jit(solution)/shard_map/while/body/eval_jaxpr/ppermute | solution.py:9
  55.0 7.7 %collective-permute-start = (bf16[256,256]{1,0:T(8,128)(2,1)S(1)}, bf16[256,256]{1,0:T(8,128)(2,1)S(1)}, u32[]{:S(2)}, u32[]{:S(2)}) collective-permute-start(bf16[256,256]{1,0:T(8,128)(2,1)S(1)} %get-tuple-element.362), channel_id=1, source_target_pairs={{0,4},{4,8},{8,12},{12,16},{16,20},{20,24},{24,28},{28,0},{1,5},{5... | collective-permute-start | bytes 393224 | tf_op jit(solution)/shard_map/while/body/eval_jaxpr/ppermute | solution.py:9
  64.4 7.7 %collective-permute-start = (bf16[256,256]{1,0:T(8,128)(2,1)S(1)}, bf16[256,256]{1,0:T(8,128)(2,1)S(1)}, u32[]{:S(2)}, u32[]{:S(2)}) collective-permute-start(bf16[256,256]{1,0:T(8,128)(2,1)S(1)} %get-tuple-element.362), channel_id=1, source_target_pairs={{0,4},{4,8},{8,12},{12,16},{16,20},{20,24},{24,28},{28,0},{1,5},{5... | collective-permute-start | bytes 393224 | tf_op jit(solution)/shard_map/while/body/eval_jaxpr/ppermute | solution.py:9
  73.8 7.7 %collective-permute-start = (bf16[256,256]{1,0:T(8,128)(2,1)S(1)}, bf16[256,256]{1,0:T(8,128)(2,1)S(1)}, u32[]{:S(2)}, u32[]{:S(2)}) collective-permute-start(bf16[256,256]{1,0:T(8,128)(2,1)S(1)} %get-tuple-element.362), channel_id=1, source_target_pairs={{0,4},{4,8},{8,12},{12,16},{16,20},{20,24},{24,28},{28,0},{1,5},{5... | collective-permute-start | bytes 393224 | tf_op jit(solution)/shard_map/while/body/eval_jaxpr/ppermute | solution.py:9
  84.0 151.9 %all-reduce.2.cloned.1.call-start = ((), (), s32[]{:S(2)}) async-start(), calls=%async_computation.2 | async-start | bytes 524288 | tf_op jit(solution)/shard_map/psum | solution.py:62
  105.8 0.9 copy-start.1
  105.8 1.0 copy-start.2
Sparse Core Ops, SparseCore 0:
  84.1 19.7 reduce-scatter.1
  110.9 124.9 all-reduce.1
where the time goes:
time: 245 us; the launch traced here: 244 us
  waiting for transfers between devices  170 us (69%)
  local copies, waits for them, and re-layouts  23.5 us (10%)
  other arithmetic  18 us (7%)
  between operations  15.3 us (6%)
  loops' own time  8.9 us (4%)
  matrix products  5.24 us (2%)
  starting transfers between devices  3.42 us (1%)
    psum x1, waiting for transfers between devices, shards(): total_grad = lax.psum(local_grad, ('blk', 'rep'))  128 us
    ppermute x7, waiting for transfers between devices, shifted(): lax.ppermute(array, axis, [(i, (i + by) % count) for i in range(count)])  21.7 us
    reduce_scatter x1, waiting for transfers between devices, shards(): lax.psum_scatter(totals.astype(jnp.bfloat16), 'rep', scatter_dimension=0,...  19.9 us
    dynamic_update_slice x16, other arithmetic, apply_panel(): lax.dynamic_update_slice_in_dim(totals, current + products[slot] * live_m...  10.5 us
    another operation x1, loops' own time, shards(): totals, _ = lax.fori_loop(1, blocks, cycle_turn, (totals, features))  8.9 us
    broadcast_in_dim x8, local copies, waits for them, and re-layouts, apply_panel(): jnp.where(index_now[..., None] == columns, weight_now[..., None], zero_we...  5.45 us
    convert_element_type x8, other arithmetic, apply_panel(): live_mask = (slot_ids < counts[panel_index]).astype(jnp.float32)  5.04 us
    dynamic_slice x8, local copies, waits for them, and re-layouts, apply_panel(): live_mask = (slot_ids < counts[panel_index]).astype(jnp.float32)  4.95 us
  transfers between devices with their start and end apart: 9, of which 9 were waited for; matrix products, arithmetic and copies ran while one was open for 9% of the time, Pallas kernels for 0%

commit v1 on v0

--- a/solution.py
+++ b/solution.py
@@ -1,6 +1,10 @@
+import functools
+
 import jax
 import jax.numpy as jnp
 from jax import lax
+from jax.experimental import pallas as pl
+from jax.experimental.pallas import tpu as pltpu
 from jax.sharding import PartitionSpec as P
 
 
@@ -65,6 +69,269 @@
     return (activations, grad_weight)
 
 
+MESH = pl.DeviceIdType.MESH
+CHUNKS = 1
+
+
+def fits(mesh):
+    blocks, reps = mesh.shape["blk"], mesh.shape["rep"]
+    return blocks % 2 == 0 and blocks * reps <= 32
+
+
+def kernel(blocks, reps, chunks, scale, feat, weight, pre, count, rowid, cols, vals, act, grad,
+           onehot, panels, pres, total, part, part_in, s1, r1, s2, r2, r3, r4,
+           x_send, x_recv, pre_send, pre_recv, p_send, p_recv,
+           g1_send, g1_recv, g2_send, g2_recv, g3_send, g3_recv, g4_send, g4_recv):
+    blk, rep = lax.axis_index("blk"), lax.axis_index("rep")
+    tile, width = feat.shape
+    part_width = width // chunks
+    depth = blocks // 2
+    x, z = lax.rem(blk, 2), blk // 2
+
+    barrier = pltpu.get_barrier_semaphore()
+    for k in range(1, blocks):
+        pl.semaphore_signal(barrier, inc=1, device_id=(lax.rem(blk + k, blocks), rep), device_id_type=MESH)
+    for k in range(1, reps):
+        pl.semaphore_signal(barrier, inc=1, device_id=(blk, lax.rem(rep + k, reps)), device_id_type=MESH)
+    for c in range(chunks):
+        panels[c, blk] = feat[:, c * part_width:(c + 1) * part_width]
+    pl.semaphore_wait(barrier, blocks + reps - 2)
+
+    def remote(src, dst, send, recv, to):
+        return pltpu.make_async_remote_copy(
+            src_ref=src, dst_ref=dst, send_sem=send, recv_sem=recv, device_id=to, device_id_type=MESH
+        )
+
+    targets = (blk + 2, blk - 2, blk + 1 - 2 * x)
+
+    def panel_copy(c, slot, way):
+        to = targets[way]
+        return remote(panels.at[c, slot], panels.at[c, slot], x_send.at[c, slot, way],
+                      x_recv.at[c, slot], (to, rep))
+
+    def order(k):
+        low = jnp.minimum(z, depth - 1 - z)
+        half = (k + 1) // 2
+        near = z - half if k % 2 == 1 else z + half
+        far = jnp.where(z < depth - 1 - z, z + (k - low), z - (k - low))
+        return jnp.where(k <= 2 * low, near, far)
+
+    def own(c):
+        pl.when(z + 1 < depth)(lambda: panel_copy(c, blk, 0).start())
+        pl.when(z > 0)(lambda: panel_copy(c, blk, 1).start())
+        panel_copy(c, blk, 2).start()
+
+    def build(p, carry):
+        rows = lax.broadcasted_iota(jnp.int32, (tile, tile), 0)
+        live = count[0, 0, p]
+        c0, c1 = cols[0, 0, p, 0], cols[0, 0, p, 1]
+        v0, v1 = vals[0, 0, p, 0].astype(jnp.float32), vals[0, 0, p, 1].astype(jnp.float32)
+        for t in range(reps):
+            first = jnp.logical_and(rowid[0, 0, p, 0] == t, live > 0)
+            second = jnp.logical_and(rowid[0, 0, p, 1] == t, live > 1)
+            value = jnp.where(first, v0, jnp.where(second, v1, 0.0))
+            index = jnp.where(first, c0, c1)
+            onehot[p, :, t * tile:(t + 1) * tile] = jnp.where(rows == index, value, 0.0).astype(jnp.bfloat16)
+        return carry
+
+    def product(c, slot):
+        return lax.dot_general(panels[c, slot], onehot[slot], (((0,), (0,)), ((), ())),
+                               preferred_element_type=jnp.float32)
+
+    def take(c, slot):
+        total[c] += product(c, slot)
+
+    def arrive(c, slot):
+        panel_copy(c, slot, 2).wait_recv()
+
+    def step(c, k):
+        where = order(k)
+        slot = where * 2 + x
+        arrive(c, slot)
+        pl.when(jnp.logical_and(where < z, z + 1 < depth))(lambda: panel_copy(c, slot, 0).start())
+        pl.when(jnp.logical_and(where > z, z > 0))(lambda: panel_copy(c, slot, 1).start())
+        panel_copy(c, slot, 2).start()
+        take(c, slot)
+        last = (z if k == 1 else order(k - 1)) * 2 + 1 - x
+        arrive(c, last)
+        take(c, last)
+
+    def to_rep(src, dst, send, recv, k):
+        return remote(src, dst, send.at[k], recv.at[rep], (blk, lax.rem(rep + k, reps)))
+
+    def from_rep(dst, send, recv, k):
+        source = lax.rem(rep + k, reps)
+        remote(dst.at[source], dst.at[source], send.at[k], recv.at[source], (blk, source)).wait_recv()
+        return source
+
+    def pre_copy(k):
+        return to_rep(pre, pres.at[rep], pre_send, pre_recv, k)
+
+    def part_copy(c, k):
+        return to_rep(part.at[c, lax.rem(rep + k, reps)], part_in.at[c, rep], p_send.at[c], p_recv.at[c], k)
+
+    own(0)
+    for k in range(1, reps):
+        pre_copy(k).start()
+    pres[rep] = pre[...]
+    lax.fori_loop(0, blocks, build, 0)
+
+    grad_rows = []
+    for c in range(chunks):
+        if c:
+            own(c)
+        total[c] = product(c, blk)
+        for k in range(1, depth):
+            step(c, k)
+        last = order(depth - 1) * 2 + 1 - x
+        arrive(c, last)
+        take(c, last)
+        for t in range(reps):
+            part[c, t] = total[c, :, t * tile:(t + 1) * tile].astype(jnp.bfloat16)
+        if c == 0:
+            for k in range(1, reps):
+                from_rep(pres, pre_send, pre_recv, k)
+        rows = jnp.dot(part[c, 0], pres[0], preferred_element_type=jnp.float32)
+        for t in range(1, reps):
+            rows += jnp.dot(part[c, t], pres[t], preferred_element_type=jnp.float32)
+        share = width // reps
+        for q in range(part_width // share):
+            s1[c * (part_width // share) + q] = rows[q * share:(q + 1) * share]
+        if c < chunks - 1:
+            for k in range(1, reps):
+                part_copy(c, k).start()
+
+    share = width // reps
+
+    def g1_copy(k):
+        return to_rep(r1.at[reps + lax.rem(rep + k, reps)], r1.at[rep], g1_send, g1_recv, k)
+
+    for q in range(reps):
+        r1[reps + q] = s1[q].astype(jnp.bfloat16)
+    for k in range(1, reps):
+        g1_copy(k).start()
+    for k in range(1, reps):
+        part_copy(chunks - 1, k).start()
+
+    mine = s1[rep]
+    for k in range(1, reps):
+        mine += r1[from_rep(r1, g1_send, g1_recv, k)].astype(jnp.float32)
+    piece = share * width // blocks // 128
+    lanes = width // 128
+    for k in range(blocks):
+        s2[k] = mine[(k // lanes) * piece:(k // lanes + 1) * piece,
+                     (k % lanes) * 128:(k % lanes + 1) * 128].astype(jnp.bfloat16)
+
+    def to_blk(src, dst, send, recv, k):
+        return remote(src, dst, send.at[k], recv.at[blk], (lax.rem(blk + k, blocks), rep))
+
+    def from_blk(dst, send, recv, k):
+        source = lax.rem(blk + k, blocks)
+        remote(dst.at[source], dst.at[source], send.at[k], recv.at[source], (source, rep)).wait_recv()
+        return source
+
+    def g2_copy(k):
+        return to_blk(s2.at[lax.rem(blk + k, blocks)], r2.at[blk], g2_send, g2_recv, k)
+
+    for k in range(1, blocks):
+        g2_copy(k).start()
+    summed = s2[blk].astype(jnp.float32)
+    for k in range(1, blocks):
+        summed += r2[from_blk(r2, g2_send, g2_recv, k)].astype(jnp.float32)
+    r3[blk] = (summed * scale).astype(jnp.bfloat16)
+
+    def g3_copy(k):
+        return to_blk(r3.at[blk], r3.at[blk], g3_send, g3_recv, k)
+
+    for k in range(1, blocks):
+        g3_copy(k).start()
+
+    preact = jnp.zeros((tile, width), jnp.float32)
+    for c in range(chunks):
+        node = part[c, rep].astype(jnp.float32)
+        for k in range(1, reps):
+            node += part_in[c, from_rep(part_in.at[c], p_send.at[c], p_recv.at[c], k)].astype(jnp.float32)
+        preact += lax.dot_general(node.astype(jnp.bfloat16), weight[c * part_width:(c + 1) * part_width],
+                                  (((0,), (0,)), ((), ())), preferred_element_type=jnp.float32)
+    act[...] = jnp.maximum(preact, 0.0).astype(jnp.bfloat16)
+
+    for k in range(1, blocks):
+        from_blk(r3, g3_send, g3_recv, k)
+
+    def g4_copy(k):
+        return to_rep(r3, r4.at[rep], g4_send, g4_recv, k)
+
+    for k in range(1, reps):
+        g4_copy(k).start()
+    r4[rep] = r3[...]
+    for c in range(chunks):
+        pl.when(z + 1 < depth)(lambda: panel_copy(c, blk, 0).wait_send())
+        pl.when(z > 0)(lambda: panel_copy(c, blk, 1).wait_send())
+        panel_copy(c, blk, 2).wait_send()
+        for k in range(1, depth):
+            where = order(k)
+            slot = where * 2 + x
+            pl.when(jnp.logical_and(where < z, z + 1 < depth))(lambda: panel_copy(c, slot, 0).wait_send())
+            pl.when(jnp.logical_and(where > z, z > 0))(lambda: panel_copy(c, slot, 1).wait_send())
+            panel_copy(c, slot, 2).wait_send()
+        for k in range(1, reps):
+            part_copy(c, k).wait_send()
+    for k in range(1, reps):
+        pre_copy(k).wait_send()
+        g1_copy(k).wait_send()
+    for k in range(1, blocks):
+        g2_copy(k).wait_send()
+        g3_copy(k).wait_send()
+    for k in range(1, reps):
+        from_rep(r4, g4_send, g4_recv, k)
+    for q in range(reps):
+        for k in range(blocks):
+            row = q * share + (k // lanes) * piece
+            grad[row:row + piece, (k % lanes) * 128:(k % lanes + 1) * 128] = r4[q, k].astype(jnp.float32)
+    for k in range(1, reps):
+        g4_copy(k).wait_send()
+
+
+def fused(features, weight, pre_cot, tile_count, tile_rowid, edge_cols, edge_vals):
+    blocks, reps = lax.axis_size("blk"), lax.axis_size("rep")
+    tile, width = features.shape
+    chunks, part_width = CHUNKS, width // CHUNKS
+    share = width // reps
+    piece = share * width // blocks // 128
+    dma = pltpu.SemaphoreType.DMA
+    vmem = pl.BlockSpec(memory_space=pltpu.VMEM)
+    smem = pl.BlockSpec(memory_space=pltpu.SMEM)
+    bf16 = jnp.bfloat16
+    scale = (blocks * reps * tile) ** (-0.5)
+    return pl.pallas_call(
+        functools.partial(kernel, blocks, reps, chunks, scale),
+        out_shape=(jax.ShapeDtypeStruct((tile, width), bf16), jax.ShapeDtypeStruct((width, width), jnp.float32)),
+        in_specs=[vmem, vmem, vmem, smem, smem, vmem, vmem],
+        out_specs=(vmem, vmem),
+        scratch_shapes=[
+            pltpu.VMEM((blocks, tile, reps * tile), bf16),
+            pltpu.VMEM((chunks, blocks, tile, part_width), bf16),
+            pltpu.VMEM((reps, tile, width), bf16),
+            pltpu.VMEM((chunks, part_width, reps * tile), jnp.float32),
+            pltpu.VMEM((chunks, reps, part_width, tile), bf16),
+            pltpu.VMEM((chunks, reps, part_width, tile), bf16),
+            pltpu.VMEM((reps, share, width), jnp.float32),
+            pltpu.VMEM((2 * reps, share, width), bf16),
+            pltpu.VMEM((blocks, piece, 128), bf16),
+            pltpu.VMEM((blocks, piece, 128), bf16),
+            pltpu.VMEM((blocks, piece, 128), bf16),
+            pltpu.VMEM((reps, blocks, piece, 128), bf16),
+            dma((chunks, blocks, 3)), dma((chunks, blocks)), dma((reps,)), dma((reps,)),
+            dma((chunks, reps)), dma((chunks, reps)),
+            dma((reps,)), dma((reps,)), dma((blocks,)), dma((blocks,)),
+            dma((blocks,)), dma((blocks,)), dma((reps,)), dma((reps,)),
+        ],
+        compiler_params=pltpu.CompilerParams(
+            collective_id=0, has_side_effects=True, vmem_limit_bytes=40 * 1024 * 1024
+        ),
+    )(features, weight, pre_cot, tile_count, tile_rowid, edge_cols, edge_vals)
+
+
 def solution(mesh):
     in_specs = (
         P(("blk", "rep"), None),
@@ -76,4 +343,5 @@
         P("blk", "rep", None, None, None, None),
     )
     out_specs = (P(("blk", "rep"), None), P())
-    return jax.shard_map(shards, mesh=mesh, in_specs=in_specs, out_specs=out_specs, check_vma=False)
+    body = fused if fits(mesh) else shards
+    return jax.shard_map(body, mesh=mesh, in_specs=in_specs, out_specs=out_specs, check_vma=False)

time: 245 us -> 46.4 us (0.19)
  waiting for transfers between devices: 170 us -> 0 us
  Pallas kernels: 0 us -> 39.9 us
  other arithmetic: 18 us -> 0 us
  local copies, waits for them, and re-layouts: 23.5 us -> 5.56 us
  between operations: 15.3 us -> 0.68 us
  loops' own time: 8.9 us -> 0 us
  matrix products: 5.24 us -> 0 us
  starting transfers between devices: 3.42 us -> 0 us
    psum x1 -> x0, waiting for transfers between devices: 128 us -> none  [shards(): total_grad = lax.psum(local_grad, ('blk', 'rep'))]
    pallas_call x0 -> x1, Pallas kernels: none -> 39.9 us  [fused(): pl.pallas_call(functools.partial(kernel, blocks, reps, chunks, scale), ou...]
    ppermute x7 -> x0, waiting for transfers between devices: 21.7 us -> none  [shifted(): lax.ppermute(array, axis, [(i, (i + by) % count) for i in range(count)])]
    reduce_scatter x1 -> x0, waiting for transfers between devices: 19.9 us -> none  [shards(): lax.psum_scatter(totals.astype(jnp.bfloat16), 'rep', scatter_dimension=0,...]
    dynamic_update_slice x16 -> x0, other arithmetic: 10.5 us -> none  [apply_panel(): lax.dynamic_update_slice_in_dim(totals, current + products[slot] * live_m...]
    slice x16 -> x0, local copies, waits for them, and re-layouts: 9.19 us -> none  [the longest x8 4.87 us: apply_panel(): live_mask[slot]]
    another operation x1 -> x0, loops' own time: 8.9 us -> none  [shards(): totals, _ = lax.fori_loop(1, blocks, cycle_turn, (totals, features))]
    convert_element_type x9 -> x0, other arithmetic: 5.9 us -> none  [the longest x8 5.04 us: apply_panel(): live_mask = (slot_ids < counts[panel_index]).astype(jnp.float32)]
  transfers between devices with their start and end apart: 9 -> 0, of which waited for: 9 -> 0; matrix products, arithmetic and copies ran while one was open for 9% -> 0% of each run, Pallas kernels for 0% -> 0%
where the time goes in v1:
time: 46.4 us; the launch traced here: 46.2 us
  Pallas kernels  39.9 us (86%)
  local copies, waits for them, and re-layouts  5.56 us (12%)
  between operations  0.68 us (1%)
    pallas_call x1, Pallas kernels, fused(): pl.pallas_call(functools.partial(kernel, blocks, reps, chunks, scale), ou...  39.9 us
    unnamed x14, local copies, waits for them, and re-layouts  5.56 us

profile of v1, /device:TPU:0, one launch (start us, length us, event | category | flops | bytes accessed | tf_op | source)
XLA Modules:
  0.0 46.2 jit_solution(6111423189125720848)
XLA Ops:
  0.6 0.0 copy-start.3
  0.6 0.8 %copy.9.rowid = s32[1,1,8,2]{3,2,1,0:T(8,128)S(1)} copy(s32[1,1,8,2]{2,3,1,0:T(2,128)} %param.11) | data formatting | bytes 128 | tf_op args[4]
  1.4 0.0 copy-start.4
  1.4 0.7 %copy.10.vals = bf16[1,1,8,2,1,256]{5,4,3,2,1,0:T(2,128)(2,1)S(1)} copy(bf16[1,1,8,2,1,256]{5,3,4,2,1,0:T(2,128)(2,1)} %param.13) | data formatting | bytes 16384 | tf_op args[6]
  2.1 0.0 copy-done.3
  2.1 0.0 copy-done.4
  2.1 0.0 copy-start
  2.2 0.9 %copy-done = bf16[256,256]{1,0:T(8,128)(2,1)S(1)} copy-done((bf16[256,256]{1,0:T(8,128)(2,1)S(1)}, bf16[256,256]{1,0:T(8,128)(2,1)}, u32[]{:S(2)}) %copy-start) | copy-done | bytes 131096
  3.1 0.0 copy-start.1
  3.1 0.9 %copy-done.1 = bf16[256,256]{1,0:T(8,128)(2,1)S(1)} copy-done((bf16[256,256]{1,0:T(8,128)(2,1)S(1)}, bf16[256,256]{1,0:T(8,128)(2,1)}, u32[]{:S(2)}) %copy-start.1) | copy-done | bytes 131096
  4.0 0.0 copy-start.2
  4.0 0.9 %copy-done.2 = bf16[256,256]{1,0:T(8,128)(2,1)S(1)} copy-done((bf16[256,256]{1,0:T(8,128)(2,1)S(1)}, bf16[256,256]{1,0:T(8,128)(2,1)}, u32[]{:S(2)}) %copy-start.2) | copy-done | bytes 131096
  4.9 39.9 %shard_map.86 = (bf16[256,256]{1,0:T(8,128)(2,1)S(1)}, f32[256,256]{1,0:T(8,128)S(1)}) custom-call(bf16[256,256]{1,0:T(8,128)(2,1)S(1)} %copy-done, bf16[256,256]{1,0:T(8,128)(2,1)S(1)} %copy-done.1, bf16[256,256]{1,0:T(8,128)(2,1)S(1)} %copy-done.2, s32[1,1,8]{2,1,0:T(1,128)S(1)} %copy-done.4, s32[1,1,8,2]{3,2,1,0:T(8,128)S(1)} %copy.9.rowid, ...), custom_call_target="tpu_custom_call" | custom-call | tf_op jit(solution)/shard_map/pallas_call | solution.py:306
  44.8 0.7 %copy.13 = bf16[256,256]{1,0:T(8,128)(2,1)} copy(bf16[256,256]{1,0:T(8,128)(2,1)S(1)} %get-tuple-element.4) | data formatting | bytes 262144
  45.5 0.7 %copy.14 = f32[256,256]{1,0:T(8,128)} copy(f32[256,256]{1,0:T(8,128)S(1)} %get-tuple-element.5) | data formatting | bytes 524288
Async XLA Ops:
  0.6 1.5 %copy-start.3 = (s32[1,1,8,2,1,256]{5,4,3,2,1,0:T(1,128)S(1)}, s32[1,1,8,2,1,256]{5,4,3,2,1,0:T(1,128)}, u32[]{:S(2)}) copy-start(s32[1,1,8,2,1,256]{5,4,3,2,1,0:T(1,128)} %cols.1) | copy-start | bytes 49156
  1.4 0.7 %copy-start.4 = (s32[1,1,8]{2,1,0:T(1,128)S(1)}, s32[1,1,8]{2,1,0:T(1,128)}, u32[]{:S(2)}) copy-start(s32[1,1,8]{2,1,0:T(1,128)} %count.1) | copy-start | bytes 100
  2.1 0.9 %copy-start = (bf16[256,256]{1,0:T(8,128)(2,1)S(1)}, bf16[256,256]{1,0:T(8,128)(2,1)}, u32[]{:S(2)}) copy-start(bf16[256,256]{1,0:T(8,128)(2,1)} %feat.1) | copy-start | bytes 393220
  3.1 0.9 %copy-start.1 = (bf16[256,256]{1,0:T(8,128)(2,1)S(1)}, bf16[256,256]{1,0:T(8,128)(2,1)}, u32[]{:S(2)}) copy-start(bf16[256,256]{1,0:T(8,128)(2,1)} %weight.1) | copy-start | bytes 393220
  4.0 0.9 %copy-start.2 = (bf16[256,256]{1,0:T(8,128)(2,1)S(1)}, bf16[256,256]{1,0:T(8,128)(2,1)}, u32[]{:S(2)}) copy-start(bf16[256,256]{1,0:T(8,128)(2,1)} %pre.1) | copy-start | bytes 393220

commit v2 on v1

--- a/solution.py
+++ b/solution.py
@@ -78,24 +78,35 @@
     return blocks % 2 == 0 and blocks * reps <= 32
 
 
-def kernel(blocks, reps, chunks, scale, feat, weight, pre, count, rowid, cols, vals, act, grad,
-           onehot, panels, pres, total, part, part_in, s1, r1, s2, r2, r3, r4,
+def kernel(blocks, reps, chunks, scale, feat, weight_in, pre_in, count, rowid, cols, vals, act, grad,
+           weight, load, onehot, panels, pres, total, part, part_in, s1, r1, s2, r2, r3, r4,
            x_send, x_recv, pre_send, pre_recv, p_send, p_recv,
-           g1_send, g1_recv, g2_send, g2_recv, g3_send, g3_recv, g4_send, g4_recv):
+           g1_send, g1_recv, g2_send, g2_recv, g3_send, g3_recv):
     blk, rep = lax.axis_index("blk"), lax.axis_index("rep")
     tile, width = feat.shape
     part_width = width // chunks
     depth = blocks // 2
     x, z = lax.rem(blk, 2), blk // 2
 
+    loads = [pltpu.make_async_copy(feat.at[:, pl.ds(c * part_width, part_width)], panels.at[c, blk], load.at[c])
+             for c in range(chunks)]
+    loads.append(pltpu.make_async_copy(pre_in, pres.at[rep], load.at[chunks]))
+    loads.append(pltpu.make_async_copy(weight_in, weight, load.at[chunks + 1]))
+    for copy in loads:
+        copy.start()
     barrier = pltpu.get_barrier_semaphore()
-    for k in range(1, blocks):
-        pl.semaphore_signal(barrier, inc=1, device_id=(lax.rem(blk + k, blocks), rep), device_id_type=MESH)
+    def greet(to):
+        pl.semaphore_signal(barrier, inc=1, device_id=(to, rep), device_id_type=MESH)
+
+    pl.when(z + 1 < depth)(lambda: greet(blk + 2))
+    pl.when(z > 0)(lambda: greet(blk - 2))
+    greet(blk + 1 - 2 * x)
     for k in range(1, reps):
         pl.semaphore_signal(barrier, inc=1, device_id=(blk, lax.rem(rep + k, reps)), device_id_type=MESH)
-    for c in range(chunks):
-        panels[c, blk] = feat[:, c * part_width:(c + 1) * part_width]
-    pl.semaphore_wait(barrier, blocks + reps - 2)
+    for copy in loads:
+        copy.wait()
+    ends = (z + 1 < depth).astype(jnp.int32) + (z > 0).astype(jnp.int32)
+    pl.semaphore_wait(barrier, reps + ends)
 
     def remote(src, dst, send, recv, to):
         return pltpu.make_async_remote_copy(
@@ -125,10 +136,11 @@
         rows = lax.broadcasted_iota(jnp.int32, (tile, tile), 0)
         live = count[0, 0, p]
         c0, c1 = cols[0, 0, p, 0], cols[0, 0, p, 1]
-        v0, v1 = vals[0, 0, p, 0].astype(jnp.float32), vals[0, 0, p, 1].astype(jnp.float32)
+        both = vals[0, 0, p, 0].astype(jnp.float32)
+        v0, v1 = both[0:1], both[1:2]
         for t in range(reps):
-            first = jnp.logical_and(rowid[0, 0, p, 0] == t, live > 0)
-            second = jnp.logical_and(rowid[0, 0, p, 1] == t, live > 1)
+            first = jnp.logical_and(rowid[0, 0, 0, p] == t, live > 0)
+            second = jnp.logical_and(rowid[0, 0, 1, p] == t, live > 1)
             value = jnp.where(first, v0, jnp.where(second, v1, 0.0))
             index = jnp.where(first, c0, c1)
             onehot[p, :, t * tile:(t + 1) * tile] = jnp.where(rows == index, value, 0.0).astype(jnp.bfloat16)
@@ -165,7 +177,7 @@
         return source
 
     def pre_copy(k):
-        return to_rep(pre, pres.at[rep], pre_send, pre_recv, k)
+        return to_rep(pres.at[rep], pres.at[rep], pre_send, pre_recv, k)
 
     def part_copy(c, k):
         return to_rep(part.at[c, lax.rem(rep + k, reps)], part_in.at[c, rep], p_send.at[c], p_recv.at[c], k)
@@ -173,7 +185,6 @@
     own(0)
     for k in range(1, reps):
         pre_copy(k).start()
-    pres[rep] = pre[...]
     lax.fori_loop(0, blocks, build, 0)
 
     grad_rows = []
@@ -240,11 +251,15 @@
         summed += r2[from_blk(r2, g2_send, g2_recv, k)].astype(jnp.float32)
     r3[blk] = (summed * scale).astype(jnp.bfloat16)
 
-    def g3_copy(k):
-        return to_blk(r3.at[blk], r3.at[blk], g3_send, g3_recv, k)
-
-    for k in range(1, blocks):
-        g3_copy(k).start()
+    others = [(i, j) for i in range(blocks) for j in range(reps) if i or j]
+
+    def g3_copy(i, j):
+        return remote(r3.at[blk], r4.at[rep, blk], g3_send.at[j, i], g3_recv.at[rep, blk],
+                      (lax.rem(blk + i, blocks), lax.rem(rep + j, reps)))
+
+    for i, j in others:
+        g3_copy(i, j).start()
+    r4[rep, blk] = r3[blk]
 
     preact = jnp.zeros((tile, width), jnp.float32)
     for c in range(chunks):
@@ -255,15 +270,6 @@
                                   (((0,), (0,)), ((), ())), preferred_element_type=jnp.float32)
     act[...] = jnp.maximum(preact, 0.0).astype(jnp.bfloat16)
 
-    for k in range(1, blocks):
-        from_blk(r3, g3_send, g3_recv, k)
-
-    def g4_copy(k):
-        return to_rep(r3, r4.at[rep], g4_send, g4_recv, k)
-
-    for k in range(1, reps):
-        g4_copy(k).start()
-    r4[rep] = r3[...]
     for c in range(chunks):
         pl.when(z + 1 < depth)(lambda: panel_copy(c, blk, 0).wait_send())
         pl.when(z > 0)(lambda: panel_copy(c, blk, 1).wait_send())
@@ -281,15 +287,12 @@
         g1_copy(k).wait_send()
     for k in range(1, blocks):
         g2_copy(k).wait_send()
-        g3_copy(k).wait_send()
-    for k in range(1, reps):
-        from_rep(r4, g4_send, g4_recv, k)
-    for q in range(reps):
-        for k in range(blocks):
-            row = q * share + (k // lanes) * piece
-            grad[row:row + piece, (k % lanes) * 128:(k % lanes + 1) * 128] = r4[q, k].astype(jnp.float32)
-    for k in range(1, reps):
-        g4_copy(k).wait_send()
+    for i, j in others:
+        b, q = lax.rem(blk + i, blocks), lax.rem(rep + j, reps)
+        remote(r4.at[q, b], r4.at[q, b], g3_send.at[j, i], g3_recv.at[q, b], (b, q)).wait_recv()
+    grad[...] = r4[...]
+    for i, j in others:
+        g3_copy(i, j).wait_send()
 
 
 def fused(features, weight, pre_cot, tile_count, tile_rowid, edge_cols, edge_vals):
@@ -300,15 +303,17 @@
     piece = share * width // blocks // 128
     dma = pltpu.SemaphoreType.DMA
     vmem = pl.BlockSpec(memory_space=pltpu.VMEM)
+    hbm = pl.BlockSpec(memory_space=pltpu.HBM)
     smem = pl.BlockSpec(memory_space=pltpu.SMEM)
     bf16 = jnp.bfloat16
     scale = (blocks * reps * tile) ** (-0.5)
-    return pl.pallas_call(
+    act, pieces = pl.pallas_call(
         functools.partial(kernel, blocks, reps, chunks, scale),
-        out_shape=(jax.ShapeDtypeStruct((tile, width), bf16), jax.ShapeDtypeStruct((width, width), jnp.float32)),
-        in_specs=[vmem, vmem, vmem, smem, smem, vmem, vmem],
+        out_shape=(jax.ShapeDtypeStruct((tile, width), bf16), jax.ShapeDtypeStruct((reps, blocks, piece, 128), bf16)),
+        in_specs=[hbm, hbm, hbm, smem, smem, vmem, vmem],
         out_specs=(vmem, vmem),
         scratch_shapes=[
+            pltpu.VMEM((width, width), bf16), dma((chunks + 2,)),
             pltpu.VMEM((blocks, tile, reps * tile), bf16),
             pltpu.VMEM((chunks, blocks, tile, part_width), bf16),
             pltpu.VMEM((reps, tile, width), bf16),
@@ -324,12 +329,15 @@
             dma((chunks, blocks, 3)), dma((chunks, blocks)), dma((reps,)), dma((reps,)),
             dma((chunks, reps)), dma((chunks, reps)),
             dma((reps,)), dma((reps,)), dma((blocks,)), dma((blocks,)),
-            dma((blocks,)), dma((blocks,)), dma((reps,)), dma((reps,)),
+            dma((reps, blocks)), dma((reps, blocks)),
         ],
         compiler_params=pltpu.CompilerParams(
-            collective_id=0, has_side_effects=True, vmem_limit_bytes=40 * 1024 * 1024
+            collective_id=0, has_side_effects=True, vmem_limit_bytes=60 * 1024 * 1024
         ),
-    )(features, weight, pre_cot, tile_count, tile_rowid, edge_cols, edge_vals)
+    )(features, weight, pre_cot, tile_count, tile_rowid.swapaxes(2, 3), edge_cols, edge_vals.swapaxes(3, 4))
+    lanes = width // 128
+    grid = pieces.reshape(reps, blocks // lanes, lanes, piece, 128).transpose(0, 1, 3, 2, 4)
+    return act, grid.reshape(width, width).astype(jnp.float32)
 
 
 def solution(mesh):

time: 46.4 us -> 41.3 us (0.89)
  local copies, waits for them, and re-layouts: 5.56 us -> 1.74 us
  Pallas kernels: 39.9 us -> 37.8 us
  other arithmetic: 0 us -> 0.92 us
    unnamed x14 -> x4, local copies, waits for them, and re-layouts: 5.56 us -> 1.6 us
    pallas_call x1, Pallas kernels: 39.9 us -> 37.8 us  [fused(): pl.pallas_call(functools.partial(kernel, blocks, reps, chunks, scale), ou...]
    convert_element_type x0 -> x1, other arithmetic: none -> 0.92 us  [fused(): return (act, grid.reshape(width, width).astype(jnp.float32))]
where the time goes in v2:
time: 41.3 us; the launch traced here: 41.1 us
  Pallas kernels  37.8 us (92%)
  local copies, waits for them, and re-layouts  1.74 us (4%)
  other arithmetic  0.92 us (2%)
  between operations  0.66 us (2%)
    pallas_call x1, Pallas kernels, fused(): pl.pallas_call(functools.partial(kernel, blocks, reps, chunks, scale), ou...  37.8 us
    unnamed x4, local copies, waits for them, and re-layouts  1.6 us
    convert_element_type x1, other arithmetic, fused(): return (act, grid.reshape(width, width).astype(jnp.float32))  0.92 us

profile of v2, /device:TPU:0, one launch (start us, length us, event | category | flops | bytes accessed | tf_op | source)
XLA Modules:
  0.0 41.1 jit_solution(12259036854618501751)
XLA Ops:
  0.6 37.8 %shard_map.86 = (bf16[256,256]{1,0:T(8,128)(2,1)}, bf16[4,8,16,128]{3,2,1,0:T(8,128)(2,1)}) custom-call(bf16[256,256]{1,0:T(8,128)(2,1)} %feat.1, bf16[256,256]{1,0:T(8,128)(2,1)} %weight_in.1, bf16[256,256]{1,0:T(8,128)(2,1)} %pre_in.1, s32[1,1,8]{2,1,0:T(1,128)} %count.1, s32[1,1,2,8]{3,2,1,0:T(2,128)} %bitcast.15, s32[1,1,8,2,1,256]{5,4,3,2,1,0:T(1,128)} %cols.1, ...), custom_call_target="tpu_custom_call" | custom-call | tf_op jit(solution)/shard_map/pallas_call | solution.py:310
  38.4 0.9 %convert_bitcast_fusion = f32[4,4,16,2,128]{4,2,3,1,0:T(8,128)S(1)} fusion(bf16[4,4,2,16,128]{4,3,2,1,0:T(8,128)(2,1)} %bitcast.13), kind=kLoop, calls=%fused_computation.1 | loop fusion | flops 65536 | bytes 393216 | tf_op jit(solution)/shard_map/convert_element_type | solution.py:340
  39.3 0.1 copy.9
  39.5 0.0 copy-start
  39.5 0.7 %copy.12 = f32[32,8,2,128]{3,1,2,0:T(8,128)} copy(f32[32,8,2,128]{3,2,1,0:T(2,128)S(1)} %bitcast.11) | data formatting | bytes 524288
  40.2 0.2 copy-done
  40.4 0.7 %copy.14 = bf16[256,256]{1,0:T(8,128)(2,1)} copy(bf16[256,256]{1,0:T(8,128)(2,1)S(1)} %copy-done) | data formatting | bytes 262144
Async XLA Ops:
  39.5 1.0 %copy-start = (bf16[256,256]{1,0:T(8,128)(2,1)S(1)}, bf16[256,256]{1,0:T(8,128)(2,1)}, u32[]{:S(2)}) copy-start(bf16[256,256]{1,0:T(8,128)(2,1)} %get-tuple-element.8) | copy-start | bytes 393220

commit v3 on v2

--- a/solution.py
+++ b/solution.py
@@ -79,9 +79,9 @@
 
 
 def kernel(blocks, reps, chunks, scale, feat, weight_in, pre_in, count, rowid, cols, vals, act, grad,
-           weight, load, onehot, panels, pres, total, part, part_in, s1, r1, s2, r2, r3, r4,
+           weight, load, onehot, panels, pres, total, part, part_in, s1, s2, r2, r3, r4,
            x_send, x_recv, pre_send, pre_recv, p_send, p_recv,
-           g1_send, g1_recv, g2_send, g2_recv, g3_send, g3_recv):
+           g2_send, g2_recv, g3_send, g3_recv):
     blk, rep = lax.axis_index("blk"), lax.axis_index("rep")
     tile, width = feat.shape
     part_width = width // chunks
@@ -213,45 +213,29 @@
                 part_copy(c, k).start()
 
     share = width // reps
-
-    def g1_copy(k):
-        return to_rep(r1.at[reps + lax.rem(rep + k, reps)], r1.at[rep], g1_send, g1_recv, k)
+    piece = share * width // blocks // 128
+    lanes = width // 128
+    others = [(i, j) for i in range(blocks) for j in range(reps) if i or j]
 
     for q in range(reps):
-        r1[reps + q] = s1[q].astype(jnp.bfloat16)
-    for k in range(1, reps):
-        g1_copy(k).start()
+        for k in range(blocks):
+            s2[q, k] = s1[q, (k // lanes) * piece:(k // lanes + 1) * piece,
+                          (k % lanes) * 128:(k % lanes + 1) * 128].astype(jnp.bfloat16)
+
+    def g2_copy(i, j):
+        b, q = lax.rem(blk + i, blocks), lax.rem(rep + j, reps)
+        return remote(s2.at[q, b], r2.at[rep, blk], g2_send.at[j, i], g2_recv.at[rep, blk], (b, q))
+
+    for i, j in others:
+        g2_copy(i, j).start()
     for k in range(1, reps):
         part_copy(chunks - 1, k).start()
-
-    mine = s1[rep]
-    for k in range(1, reps):
-        mine += r1[from_rep(r1, g1_send, g1_recv, k)].astype(jnp.float32)
-    piece = share * width // blocks // 128
-    lanes = width // 128
-    for k in range(blocks):
-        s2[k] = mine[(k // lanes) * piece:(k // lanes + 1) * piece,
-                     (k % lanes) * 128:(k % lanes + 1) * 128].astype(jnp.bfloat16)
-
-    def to_blk(src, dst, send, recv, k):
-        return remote(src, dst, send.at[k], recv.at[blk], (lax.rem(blk + k, blocks), rep))
-
-    def from_blk(dst, send, recv, k):
-        source = lax.rem(blk + k, blocks)
-        remote(dst.at[source], dst.at[source], send.at[k], recv.at[source], (source, rep)).wait_recv()
-        return source
-
-    def g2_copy(k):
-        return to_blk(s2.at[lax.rem(blk + k, blocks)], r2.at[blk], g2_send, g2_recv, k)
-
-    for k in range(1, blocks):
-        g2_copy(k).start()
-    summed = s2[blk].astype(jnp.float32)
-    for k in range(1, blocks):
-        summed += r2[from_blk(r2, g2_send, g2_recv, k)].astype(jnp.float32)
+    summed = s2[rep, blk].astype(jnp.float32)
+    for i, j in others:
+        b, q = lax.rem(blk + i, blocks), lax.rem(rep + j, reps)
+        remote(r2.at[q, b], r2.at[q, b], g2_send.at[j, i], g2_recv.at[q, b], (b, q)).wait_recv()
+        summed += r2[q, b].astype(jnp.float32)
     r3[blk] = (summed * scale).astype(jnp.bfloat16)
-
-    others = [(i, j) for i in range(blocks) for j in range(reps) if i or j]
 
     def g3_copy(i, j):
         return remote(r3.at[blk], r4.at[rep, blk], g3_send.at[j, i], g3_recv.at[rep, blk],
@@ -284,9 +268,8 @@
             part_copy(c, k).wait_send()
     for k in range(1, reps):
         pre_copy(k).wait_send()
-        g1_copy(k).wait_send()
-    for k in range(1, blocks):
-        g2_copy(k).wait_send()
+    for i, j in others:
+        g2_copy(i, j).wait_send()
     for i, j in others:
         b, q = lax.rem(blk + i, blocks), lax.rem(rep + j, reps)
         remote(r4.at[q, b], r4.at[q, b], g3_send.at[j, i], g3_recv.at[q, b], (b, q)).wait_recv()
@@ -321,14 +304,13 @@
             pltpu.VMEM((chunks, reps, part_width, tile), bf16),
             pltpu.VMEM((chunks, reps, part_width, tile), bf16),
             pltpu.VMEM((reps, share, width), jnp.float32),
-            pltpu.VMEM((2 * reps, share, width), bf16),
-            pltpu.VMEM((blocks, piece, 128), bf16),
-            pltpu.VMEM((blocks, piece, 128), bf16),
+            pltpu.VMEM((reps, blocks, piece, 128), bf16),
+            pltpu.VMEM((reps, blocks, piece, 128), bf16),
             pltpu.VMEM((blocks, piece, 128), bf16),
             pltpu.VMEM((reps, blocks, piece, 128), bf16),
             dma((chunks, blocks, 3)), dma((chunks, blocks)), dma((reps,)), dma((reps,)),
             dma((chunks, reps)), dma((chunks, reps)),
-            dma((reps,)), dma((reps,)), dma((blocks,)), dma((blocks,)),
+            dma((reps, blocks)), dma((reps, blocks)),
             dma((reps, blocks)), dma((reps, blocks)),
         ],
         compiler_params=pltpu.CompilerParams(

time: 41.3 us -> 40.1 us (0.971)
  Pallas kernels: 37.8 us -> 36.6 us
    pallas_call x1, Pallas kernels: 37.8 us -> 36.6 us  [fused(): pl.pallas_call(functools.partial(kernel, blocks, reps, chunks, scale), ou...]
where the time goes in v3:
time: 40.1 us; the launch traced here: 39.9 us
  Pallas kernels  36.6 us (91%)
  local copies, waits for them, and re-layouts  1.74 us (4%)
  other arithmetic  0.92 us (2%)
  between operations  0.66 us (2%)
    pallas_call x1, Pallas kernels, fused(): pl.pallas_call(functools.partial(kernel, blocks, reps, chunks, scale), ou...  36.6 us
    unnamed x4, local copies, waits for them, and re-layouts  1.6 us
    convert_element_type x1, other arithmetic, fused(): return (act, grid.reshape(width, width).astype(jnp.float32))  0.92 us

profile of v3, /device:TPU:0, one launch (start us, length us, event | category | flops | bytes accessed | tf_op | source)
XLA Modules:
  0.0 39.9 jit_solution(12921941826459143737)
XLA Ops:
  0.6 36.6 %shard_map.86 = (bf16[256,256]{1,0:T(8,128)(2,1)}, bf16[4,8,16,128]{3,2,1,0:T(8,128)(2,1)}) custom-call(bf16[256,256]{1,0:T(8,128)(2,1)} %feat.1, bf16[256,256]{1,0:T(8,128)(2,1)} %weight_in.1, bf16[256,256]{1,0:T(8,128)(2,1)} %pre_in.1, s32[1,1,8]{2,1,0:T(1,128)} %count.1, s32[1,1,2,8]{3,2,1,0:T(2,128)} %bitcast.15, s32[1,1,8,2,1,256]{5,4,3,2,1,0:T(1,128)} %cols.1, ...), custom_call_target="tpu_custom_call" | custom-call | tf_op jit(solution)/shard_map/pallas_call | solution.py:293
  37.2 0.9 %convert_bitcast_fusion = f32[4,4,16,2,128]{4,2,3,1,0:T(8,128)S(1)} fusion(bf16[4,4,2,16,128]{4,3,2,1,0:T(8,128)(2,1)} %bitcast.13), kind=kLoop, calls=%fused_computation.1 | loop fusion | flops 65536 | bytes 393216 | tf_op jit(solution)/shard_map/convert_element_type | solution.py:322
  38.2 0.1 copy.9
  38.3 0.0 copy-start
  38.3 0.7 %copy.12 = f32[32,8,2,128]{3,1,2,0:T(8,128)} copy(f32[32,8,2,128]{3,2,1,0:T(2,128)S(1)} %bitcast.11) | data formatting | bytes 524288
  39.0 0.2 copy-done
  39.3 0.7 %copy.14 = bf16[256,256]{1,0:T(8,128)(2,1)} copy(bf16[256,256]{1,0:T(8,128)(2,1)S(1)} %copy-done) | data formatting | bytes 262144
Async XLA Ops:
  38.3 1.0 %copy-start = (bf16[256,256]{1,0:T(8,128)(2,1)S(1)}, bf16[256,256]{1,0:T(8,128)(2,1)}, u32[]{:S(2)}) copy-start(bf16[256,256]{1,0:T(8,128)(2,1)} %get-tuple-element.8) | copy-start | bytes 393220

commit v4 on v3

--- a/solution.py
+++ b/solution.py
@@ -71,6 +71,7 @@
 
 MESH = pl.DeviceIdType.MESH
 CHUNKS = 1
+HALVES = 2
 
 
 def fits(mesh):
@@ -115,10 +116,10 @@
 
     targets = (blk + 2, blk - 2, blk + 1 - 2 * x)
 
-    def panel_copy(c, slot, way):
-        to = targets[way]
-        return remote(panels.at[c, slot], panels.at[c, slot], x_send.at[c, slot, way],
-                      x_recv.at[c, slot], (to, rep))
+    def panel_copy(c, slot, way, half):
+        rows = panels.at[c, slot, pl.ds(half * (tile // HALVES), tile // HALVES)]
+        return remote(rows, rows, x_send.at[c, slot, way, half],
+                      x_recv.at[c, slot, half], (targets[way], rep))
 
     def order(k):
         low = jnp.minimum(z, depth - 1 - z)
@@ -128,9 +129,10 @@
         return jnp.where(k <= 2 * low, near, far)
 
     def own(c):
-        pl.when(z + 1 < depth)(lambda: panel_copy(c, blk, 0).start())
-        pl.when(z > 0)(lambda: panel_copy(c, blk, 1).start())
-        panel_copy(c, blk, 2).start()
+        for h in range(HALVES):
+            pl.when(z + 1 < depth)(lambda: panel_copy(c, blk, 0, h).start())
+            pl.when(z > 0)(lambda: panel_copy(c, blk, 1, h).start())
+            panel_copy(c, blk, 2, h).start()
 
     def build(p, carry):
         rows = lax.broadcasted_iota(jnp.int32, (tile, tile), 0)
@@ -154,15 +156,17 @@
         total[c] += product(c, slot)
 
     def arrive(c, slot):
-        panel_copy(c, slot, 2).wait_recv()
+        for h in range(HALVES):
+            panel_copy(c, slot, 2, h).wait_recv()
 
     def step(c, k):
         where = order(k)
         slot = where * 2 + x
-        arrive(c, slot)
-        pl.when(jnp.logical_and(where < z, z + 1 < depth))(lambda: panel_copy(c, slot, 0).start())
-        pl.when(jnp.logical_and(where > z, z > 0))(lambda: panel_copy(c, slot, 1).start())
-        panel_copy(c, slot, 2).start()
+        for h in range(HALVES):
+            panel_copy(c, slot, 2, h).wait_recv()
+            pl.when(jnp.logical_and(where < z, z + 1 < depth))(lambda: panel_copy(c, slot, 0, h).start())
+            pl.when(jnp.logical_and(where > z, z > 0))(lambda: panel_copy(c, slot, 1, h).start())
+            panel_copy(c, slot, 2, h).start()
         take(c, slot)
         last = (z if k == 1 else order(k - 1)) * 2 + 1 - x
         arrive(c, last)
@@ -255,15 +259,16 @@
     act[...] = jnp.maximum(preact, 0.0).astype(jnp.bfloat16)
 
     for c in range(chunks):
-        pl.when(z + 1 < depth)(lambda: panel_copy(c, blk, 0).wait_send())
-        pl.when(z > 0)(lambda: panel_copy(c, blk, 1).wait_send())
-        panel_copy(c, blk, 2).wait_send()
-        for k in range(1, depth):
-            where = order(k)
-            slot = where * 2 + x
-            pl.when(jnp.logical_and(where < z, z + 1 < depth))(lambda: panel_copy(c, slot, 0).wait_send())
-            pl.when(jnp.logical_and(where > z, z > 0))(lambda: panel_copy(c, slot, 1).wait_send())
-            panel_copy(c, slot, 2).wait_send()
+        for h in range(HALVES):
+            pl.when(z + 1 < depth)(lambda: panel_copy(c, blk, 0, h).wait_send())
+            pl.when(z > 0)(lambda: panel_copy(c, blk, 1, h).wait_send())
+            panel_copy(c, blk, 2, h).wait_send()
+            for k in range(1, depth):
+                where = order(k)
+                slot = where * 2 + x
+                pl.when(jnp.logical_and(where < z, z + 1 < depth))(lambda: panel_copy(c, slot, 0, h).wait_send())
+                pl.when(jnp.logical_and(where > z, z > 0))(lambda: panel_copy(c, slot, 1, h).wait_send())
+                panel_copy(c, slot, 2, h).wait_send()
         for k in range(1, reps):
             part_copy(c, k).wait_send()
     for k in range(1, reps):
@@ -308,7 +313,7 @@
             pltpu.VMEM((reps, blocks, piece, 128), bf16),
             pltpu.VMEM((blocks, piece, 128), bf16),
             pltpu.VMEM((reps, blocks, piece, 128), bf16),
-            dma((chunks, blocks, 3)), dma((chunks, blocks)), dma((reps,)), dma((reps,)),
+            dma((chunks, blocks, 3, HALVES)), dma((chunks, blocks, HALVES)), dma((reps,)), dma((reps,)),
             dma((chunks, reps)), dma((chunks, reps)),
             dma((reps, blocks)), dma((reps, blocks)),
             dma((reps, blocks)), dma((reps, blocks)),

time: 40.1 us -> 38.4 us (0.958)
  Pallas kernels: 36.6 us -> 34.8 us
    pallas_call x1, Pallas kernels: 36.6 us -> 34.8 us  [fused(): pl.pallas_call(functools.partial(kernel, blocks, reps, chunks, scale), ou...]
where the time goes in v4:
time: 38.4 us; the launch traced here: 38.2 us
  Pallas kernels  34.8 us (91%)
  local copies, waits for them, and re-layouts  1.74 us (5%)
  other arithmetic  0.92 us (2%)
  between operations  0.66 us (2%)
    pallas_call x1, Pallas kernels, fused(): pl.pallas_call(functools.partial(kernel, blocks, reps, chunks, scale), ou...  34.8 us
    unnamed x4, local copies, waits for them, and re-layouts  1.6 us
    convert_element_type x1, other arithmetic, fused(): return (act, grid.reshape(width, width).astype(jnp.float32))  0.92 us

profile of v4, /device:TPU:0, one launch (start us, length us, event | category | flops | bytes accessed | tf_op | source)
XLA Modules:
  0.0 38.2 jit_solution(9018561967600872992)
XLA Ops:
  0.6 34.8 %shard_map.86 = (bf16[256,256]{1,0:T(8,128)(2,1)}, bf16[4,8,16,128]{3,2,1,0:T(8,128)(2,1)}) custom-call(bf16[256,256]{1,0:T(8,128)(2,1)} %feat.1, bf16[256,256]{1,0:T(8,128)(2,1)} %weight_in.1, bf16[256,256]{1,0:T(8,128)(2,1)} %pre_in.1, s32[1,1,8]{2,1,0:T(1,128)} %count.1, s32[1,1,2,8]{3,2,1,0:T(2,128)} %bitcast.15, s32[1,1,8,2,1,256]{5,4,3,2,1,0:T(1,128)} %cols.1, ...), custom_call_target="tpu_custom_call" | custom-call | tf_op jit(solution)/shard_map/pallas_call | solution.py:298
  35.5 0.9 %convert_bitcast_fusion = f32[4,4,16,2,128]{4,2,3,1,0:T(8,128)S(1)} fusion(bf16[4,4,2,16,128]{4,3,2,1,0:T(8,128)(2,1)} %bitcast.13), kind=kLoop, calls=%fused_computation.1 | loop fusion | flops 65536 | bytes 393216 | tf_op jit(solution)/shard_map/convert_element_type | solution.py:327
  36.4 0.1 copy.9
  36.5 0.0 copy-start
  36.6 0.7 %copy.12 = f32[32,8,2,128]{3,1,2,0:T(8,128)} copy(f32[32,8,2,128]{3,2,1,0:T(2,128)S(1)} %bitcast.11) | data formatting | bytes 524288
  37.3 0.2 copy-done
  37.5 0.7 %copy.14 = bf16[256,256]{1,0:T(8,128)(2,1)} copy(bf16[256,256]{1,0:T(8,128)(2,1)S(1)} %copy-done) | data formatting | bytes 262144
Async XLA Ops:
  36.5 1.0 %copy-start = (bf16[256,256]{1,0:T(8,128)(2,1)S(1)}, bf16[256,256]{1,0:T(8,128)(2,1)}, u32[]{:S(2)}) copy-start(bf16[256,256]{1,0:T(8,128)(2,1)} %get-tuple-element.8) | copy-start | bytes 393220

commit v5 on v4

--- a/solution.py
+++ b/solution.py
@@ -71,7 +71,7 @@
 
 MESH = pl.DeviceIdType.MESH
 CHUNKS = 1
-HALVES = 2
+HALVES = 4
 
 
 def fits(mesh):

time: 38.4 us -> 38.5 us (level)
  no operation moved by 1% of the time
where the time goes in v5:
time: 38.5 us; the launch traced here: 38.3 us
  Pallas kernels  34.9 us (91%)
  local copies, waits for them, and re-layouts  1.74 us (5%)
  other arithmetic  0.92 us (2%)
  between operations  0.66 us (2%)
    pallas_call x1, Pallas kernels, fused(): pl.pallas_call(functools.partial(kernel, blocks, reps, chunks, scale), ou...  34.9 us
    unnamed x4, local copies, waits for them, and re-layouts  1.6 us
    convert_element_type x1, other arithmetic, fused(): return (act, grid.reshape(width, width).astype(jnp.float32))  0.92 us

profile of v5, /device:TPU:0, one launch (start us, length us, event | category | flops | bytes accessed | tf_op | source)
XLA Modules:
  0.0 38.3 jit_solution(2407766763372991063)
XLA Ops:
  0.6 34.9 %shard_map.86 = (bf16[256,256]{1,0:T(8,128)(2,1)}, bf16[4,8,16,128]{3,2,1,0:T(8,128)(2,1)}) custom-call(bf16[256,256]{1,0:T(8,128)(2,1)} %feat.1, bf16[256,256]{1,0:T(8,128)(2,1)} %weight_in.1, bf16[256,256]{1,0:T(8,128)(2,1)} %pre_in.1, s32[1,1,8]{2,1,0:T(1,128)} %count.1, s32[1,1,2,8]{3,2,1,0:T(2,128)} %bitcast.15, s32[1,1,8,2,1,256]{5,4,3,2,1,0:T(1,128)} %cols.1, ...), custom_call_target="tpu_custom_call" | custom-call | tf_op jit(solution)/shard_map/pallas_call | solution.py:298
  35.6 0.9 %convert_bitcast_fusion = f32[4,4,16,2,128]{4,2,3,1,0:T(8,128)S(1)} fusion(bf16[4,4,2,16,128]{4,3,2,1,0:T(8,128)(2,1)} %bitcast.13), kind=kLoop, calls=%fused_computation.1 | loop fusion | flops 65536 | bytes 393216 | tf_op jit(solution)/shard_map/convert_element_type | solution.py:327
  36.5 0.1 copy.9
  36.6 0.0 copy-start
  36.7 0.7 %copy.12 = f32[32,8,2,128]{3,1,2,0:T(8,128)} copy(f32[32,8,2,128]{3,2,1,0:T(2,128)S(1)} %bitcast.11) | data formatting | bytes 524288
  37.4 0.2 copy-done
  37.6 0.7 %copy.14 = bf16[256,256]{1,0:T(8,128)(2,1)} copy(bf16[256,256]{1,0:T(8,128)(2,1)S(1)} %copy-done) | data formatting | bytes 262144
Async XLA Ops:
  36.6 1.0 %copy-start = (bf16[256,256]{1,0:T(8,128)(2,1)S(1)}, bf16[256,256]{1,0:T(8,128)(2,1)}, u32[]{:S(2)}) copy-start(bf16[256,256]{1,0:T(8,128)(2,1)} %get-tuple-element.8) | copy-start | bytes 393220
